TPU v7x, 128 devices: a whole 4x4x4 slice. The times are simulated.
128 devices in a mesh: row: 16 (over y_lo, z, core), col: 8 (over x, y_hi).
Axes of the slice: x: 4, y: 4 (y_hi: 2, y_lo: 2; y = y_hi * 2 + y_lo), z: 4, core: 2. Of those that a mesh axis runs over, the one named last changes fastest.
Arguments:
- out_cotangent: bfloat16 [2048, 8192], P('row', 'col'), may hold values from -1.25 to 1.25
- saved_input: bfloat16 [2048, 8192], P('row', 'col'), may hold values from -6 to 6
- scan_output: bfloat16 [2048, 16384], P('col', 'row'), may hold values from -6 to 6
- gate_input: bfloat16 [2048, 16384], P('col', 'row'), may hold values from -8 to 8
- branch_grad: bfloat16 [2048, 16384], P('col', 'row'), may hold values from -1.25 to 1.25
- out_weight: bfloat16 [16384, 8192], P('row', 'col'), may hold values from -0.046875 to 0.046875
- in_weight: bfloat16 [8192, 2, 16384], P('col', None, 'row'), may hold values from -0.0625 to 0.0625
Outputs:
- input_grad: bfloat16 [2048, 8192], P('row', 'col')
- scan_grad: bfloat16 [2048, 16384], P('col', 'row')
- in_weight_grad: float32 [8192, 2, 16384], P('col', None, 'row')
- out_weight_grad: float32 [16384, 8192], P('row', 'col')
All inputs are finite; a program needn't handle non-finite values.
Results may differ from a plain program's by a relative error of at most 0.025.
Values may be sent and summed in bfloat16 or wider, within the bound.
A program may use at most 192 MiB of HBM per device.

v0:
```python
import jax
import jax.numpy as jnp
from jax import lax
from jax.sharding import PartitionSpec as P


def gate_backward(summed, scan_output, gate_input):
    gate_value = gate_input.astype(jnp.float32)
    sigmoid_gate = jax.nn.sigmoid(gate_value)
    silu_gate = gate_value * sigmoid_gate
    scan_value = scan_output.astype(jnp.float32)
    gated = (scan_value * silu_gate).astype(jnp.bfloat16)
    gate_grad = (
        summed * scan_value * sigmoid_gate * (1.0 + gate_value * (1.0 - sigmoid_gate))
    ).astype(jnp.bfloat16)
    scan_grad = (summed * silu_gate).astype(jnp.bfloat16)
    return (gated, gate_grad, scan_grad)


def per_device(
    out_cotangent, saved_input, scan_output, gate_input, branch_grad, out_weight, in_weight
):
    cotangent = lax.all_gather(out_cotangent, "row", axis=0, tiled=True)
    shares = lax.psum_scatter(
        lax.dot_general(
            cotangent, out_weight, (((1,), (1,)), ((), ())), preferred_element_type=jnp.float32
        ).astype(jnp.bfloat16),
        "col",
        scatter_dimension=0,
        tiled=True,
    ).astype(jnp.float32)
    gated, gate_grad, scan_grad = gate_backward(shares, scan_output, gate_input)
    gated_all, branch_all, gate_grad_all = (
        lax.all_gather(gated, "col", axis=0, tiled=True),
        lax.all_gather(branch_grad, "col", axis=0, tiled=True),
        lax.all_gather(gate_grad, "col", axis=0, tiled=True),
    )
    out_weight_grad = lax.dot_general(
        gated_all, cotangent, (((0,), (0,)), ((), ())), preferred_element_type=jnp.float32
    )
    branch_weight = in_weight[:, 0, :]
    gate_weight = in_weight[:, 1, :]
    branch_rows = branch_all
    gate_rows = gate_grad_all
    total = lax.dot_general(
        branch_rows, branch_weight, (((1,), (1,)), ((), ())), preferred_element_type=jnp.float32
    )
    input_grad = lax.psum_scatter(
        (
            total
            + lax.dot_general(
                gate_rows, gate_weight, (((1,), (1,)), ((), ())), preferred_element_type=jnp.float32
            )
        ).astype(jnp.bfloat16),
        "row",
        scatter_dimension=0,
        tiled=True,
    )
    piece = lax.all_gather(saved_input, "row", axis=0, tiled=True)
    branch_rows = branch_all
    gate_rows = gate_grad_all
    branch_sum = lax.dot_general(
        piece, branch_rows, (((0,), (0,)), ((), ())), preferred_element_type=jnp.float32
    )
    gate_sum = lax.dot_general(
        piece, gate_rows, (((0,), (0,)), ((), ())), preferred_element_type=jnp.float32
    )
    in_weight_grad = jnp.stack([branch_sum, gate_sum], axis=1)
    return (input_grad, scan_grad, in_weight_grad, out_weight_grad)


def solution(mesh):
    return jax.shard_map(
        per_device,
        mesh=mesh,
        in_specs=(
            P("row", "col"),
            P("row", "col"),
            P("col", "row"),
            P("col", "row"),
            P("col", "row"),
            P("row", "col"),
            P("col", None, "row"),
        ),
        out_specs=(P("row", "col"), P("col", "row"), P("col", None, "row"), P("row", "col")),
        check_vma=False,
    )
```

profile of v0, /device:TPU:6, one launch (start us, length us, event | category | flops | bytes accessed | tf_op | source)
XLA Modules:
  0.0 472.9 jit_solution(15257157116937590052)
XLA Ops:
  7.2 0.0 copy-start
  7.2 0.0 all-gather.8.cloned.1.call-start
  7.2 0.7 all-gather.8.cloned.1.call-update
  7.9 0.0 reduce-scatter.3.cloned.1.call-start
  8.0 41.6 %all-gather.8.cloned.1.call-done = bf16[2048,1024]{1,0:T(8,128)(2,1)} async-done(((bf16[128,1024]{1,0:T(8,128)(2,1)}), bf16[2048,1024]{1,0:T(8,128)(2,1)}) %all-gather.8.cloned.1.call-update) | async-done | bytes 4194320 | tf_op jit(solution)/shard_map/all_gather | solution.py:23
  49.5 0.0 copy-done
  49.5 8.3 %convolution_convert_fusion = bf16[2048,1024]{1,0:T(8,128)(2,1)} fusion(bf16[2048,1024]{1,0:T(8,128)(2,1)} %all-gather.8.cloned.1.call-done, bf16[1024,1024]{1,0:T(8,128)(2,1)S(1)} %copy-done), kind=kOutput, calls=%fused_computation.2 | convolution fusion | flops 4297064448 | bytes 10485760 | tf_op jit(solution)/shard_map/dot_general | solution.py:25
  57.8 0.0 copy-start.2
  57.8 0.0 copy-start.3
  57.8 0.0 reduce-scatter.3.cloned.1.call-update
  57.8 0.0 all-gather.6.cloned.1.call-start
  57.9 0.7 all-gather.6.cloned.1.call-update
  58.6 0.0 all-gather.10.cloned.1.call-start
  58.6 84.0 %reduce-scatter.3.cloned.1.call-done = bf16[256,1024]{1,0:T(8,128)(2,1)} async-done(((bf16[2048,1024]{1,0:T(8,128)(2,1)}), bf16[256,1024]{1,0:T(8,128)(2,1)}) %reduce-scatter.3.cloned.1.call-update) | async-done | bytes 524304 | tf_op jit(solution)/shard_map/reduce_scatter | solution.py:24
  142.7 0.0 copy-done.2
  142.7 0.0 copy-done.3
  142.7 3.0 fusion.5
  145.6 0.0 all-gather.10.cloned.1.call-update
  145.6 0.0 all-gather.12.cloned.1.call-start
  145.7 0.5 all-gather.12.cloned.1.call-update
  146.2 0.0 all-gather.14.cloned.1.call-start
  146.3 0.5 all-gather.14.cloned.1.call-update
  146.8 0.2 reduce-scatter.5.cloned.1.call-start
  147.0 9.8 %fusion.10 = (bf16[1024,1,1024]{2,1,0:T(2,128)(2,1)}, bf16[1024,1,1024]{2,1,0:T(2,128)(2,1)}) fusion(bf16[1024,2,1024]{2,1,0:T(2,128)(2,1)} %param.13), kind=kLoop, calls=%fused_computation.23 | loop fusion | bytes 8388608 | tf_op jit(solution)/shard_map/slice | solution.py:42
  156.8 57.0 %all-gather.6.cloned.1.call-done = bf16[2048,1024]{1,0:T(8,128)(2,1)} async-done(((bf16[256,1024]{1,0:T(8,128)(2,1)}), bf16[2048,1024]{1,0:T(8,128)(2,1)}) %all-gather.6.cloned.1.call-update) | async-done | bytes 4194320 | tf_op jit(solution)/shard_map/all_gather | solution.py:35
  213.8 11.4 %fusion = f32[2048,1024]{1,0:T(8,128)} fusion(bf16[2048,1024]{1,0:T(8,128)(2,1)} %all-gather.6.cloned.1.call-done, bf16[1024,1,1024]{2,1,0:T(2,128)(2,1)} %get-tuple-element.13), kind=kOutput, calls=%fused_computation.7 | convolution fusion | flops 4294967296 | bytes 14680064 | tf_op jit(solution)/shard_map/dot_general | solution.py:45
  225.2 60.2 %all-gather.10.cloned.1.call-done = bf16[2048,1024]{1,0:T(8,128)(2,1)} async-done(((bf16[256,1024]{1,0:T(8,128)(2,1)}), bf16[2048,1024]{1,0:T(8,128)(2,1)}) %all-gather.10.cloned.1.call-update) | async-done | bytes 4194320 | tf_op jit(solution)/shard_map/all_gather | solution.py:36
  285.4 12.5 %add_convert_fusion = bf16[2048,1024]{1,0:T(8,128)(2,1)} fusion(f32[2048,1024]{1,0:T(8,128)} %fusion, bf16[2048,1024]{1,0:T(8,128)(2,1)} %all-gather.10.cloned.1.call-done, bf16[1024,1,1024]{2,1,0:T(2,128)(2,1)} %get-tuple-element.12), kind=kOutput, calls=%fused_computation.1 | convolution fusion | flops 4299161600 | bytes 18874368 | tf_op jit(solution)/shard_map/dot_general | solution.py:51
  297.9 0.0 reduce-scatter.5.cloned.1.call-update
  297.9 26.3 %all-gather.12.cloned.1.call-done = bf16[2048,1024]{1,0:T(8,128)(2,1)} async-done(((bf16[128,1024]{1,0:T(8,128)(2,1)}), bf16[2048,1024]{1,0:T(8,128)(2,1)}) %all-gather.12.cloned.1.call-update) | async-done | bytes 4194320 | tf_op jit(solution)/shard_map/all_gather | solution.py:59
  324.2 0.0 copy-start.4
  324.3 0.0 copy-start.5
  324.3 7.9 %convolution_bitcast_fusion.1 = f32[1024,1,1024]{2,0,1:T(8,128)S(1)} fusion(bf16[2048,1024]{1,0:T(8,128)(2,1)} %all-gather.12.cloned.1.call-done, bf16[2048,1024]{1,0:T(8,128)(2,1)} %all-gather.6.cloned.1.call-done), kind=kOutput, calls=%fused_computation.4 | convolution fusion | flops 4294967296 | bytes 12582912 | tf_op jit(solution)/shard_map/dot_general | solution.py:62
  332.2 0.0 copy-done.4
  332.2 0.0 copy-done.5
  332.2 4.7 %convolution_bitcast_fusion = f32[1024,1,1024]{2,0,1:T(8,128)S(1)} fusion(bf16[2048,1024]{1,0:T(8,128)(2,1)S(1)} %copy-done.4, bf16[2048,1024]{1,0:T(8,128)(2,1)S(1)} %copy-done.5), kind=kOutput, calls=%fused_computation.3 | convolution fusion | flops 4294967296 | bytes 12582912 | tf_op jit(solution)/shard_map/dot_general | solution.py:65
  337.0 1.7 pad_maximum_fusion
  338.6 12.9 %copy.16 = f32[1024,2,1024]{2,1,0:T(2,128)} copy(f32[1024,2,1024]{2,0,1:T(8,128)S(1)} %pad_maximum_fusion) | data formatting | bytes 16777216
  351.6 44.6 %all-gather.14.cloned.1.call-done = bf16[2048,1024]{1,0:T(8,128)(2,1)} async-done(((bf16[256,1024]{1,0:T(8,128)(2,1)}), bf16[2048,1024]{1,0:T(8,128)(2,1)}) %all-gather.14.cloned.1.call-update) | async-done | bytes 4194320 | tf_op jit(solution)/shard_map/all_gather | solution.py:34
  396.1 0.0 copy-start.1
  396.1 10.2 %fusion.11 = f32[1024,1024]{1,0:T(8,128)} fusion(bf16[2048,1024]{1,0:T(8,128)(2,1)} %all-gather.14.cloned.1.call-done, bf16[2048,1024]{1,0:T(8,128)(2,1)} %all-gather.8.cloned.1.call-done), kind=kOutput, calls=%fused_computation.24 | convolution fusion | flops 4294967296 | bytes 12582912 | tf_op jit(solution)/shard_map/dot_general | solution.py:38
  406.3 59.7 %reduce-scatter.5.cloned.1.call-done = bf16[128,1024]{1,0:T(8,128)(2,1)} async-done(((bf16[2048,1024]{1,0:T(8,128)(2,1)}), bf16[128,1024]{1,0:T(8,128)(2,1)}) %reduce-scatter.5.cloned.1.call-update) | async-done | bytes 262160 | tf_op jit(solution)/shard_map/reduce_scatter | solution.py:48
  466.0 0.0 copy-done.1
Async XLA Ops:
  7.2 42.4 %copy-start = (bf16[1024,1024]{1,0:T(8,128)(2,1)S(1)}, bf16[1024,1024]{1,0:T(8,128)(2,1)}, u32[]{:S(2)}) copy-start(bf16[1024,1024]{1,0:T(8,128)(2,1)} %param.12) | copy-start | bytes 6291460
  7.2 42.3 %all-gather.8.cloned.1.call-start = ((), (), s32[]{:S(2)}) async-start(), calls=%async_computation.3 | async-start | bytes 4456448 | tf_op jit(solution)/shard_map/all_gather | solution.py:23
  7.9 134.7 %reduce-scatter.3.cloned.1.call-start = ((), (), s32[]{:S(2)}) async-start(), calls=%async_computation.4 | async-start | bytes 4718592 | tf_op jit(solution)/shard_map/reduce_scatter | solution.py:24
  57.8 84.9 %copy-start.2 = (bf16[256,1024]{1,0:T(8,128)(2,1)S(1)}, bf16[256,1024]{1,0:T(8,128)(2,1)}, u32[]{:S(2)}) copy-start(bf16[256,1024]{1,0:T(8,128)(2,1)} %param.9) | copy-start | bytes 1572868
  57.8 84.9 %copy-start.3 = (bf16[256,1024]{1,0:T(8,128)(2,1)S(1)}, bf16[256,1024]{1,0:T(8,128)(2,1)}, u32[]{:S(2)}) copy-start(bf16[256,1024]{1,0:T(8,128)(2,1)} %param.10) | copy-start | bytes 1572868
  57.8 155.9 %all-gather.6.cloned.1.call-start = ((), (), s32[]{:S(2)}) async-start(), calls=%async_computation.2 | async-start | bytes 4718592 | tf_op jit(solution)/shard_map/all_gather | solution.py:35
  58.6 226.9 %all-gather.10.cloned.1.call-start = ((), (), s32[]{:S(2)}) async-start(), calls=%async_computation.5 | async-start | bytes 4718592 | tf_op jit(solution)/shard_map/all_gather | solution.py:36
  145.6 178.6 %all-gather.12.cloned.1.call-start = ((), (), s32[]{:S(2)}) async-start(), calls=%async_computation.7 | async-start | bytes 4456448 | tf_op jit(solution)/shard_map/all_gather | solution.py:59
  146.2 249.9 %all-gather.14.cloned.1.call-start = ((), (), s32[]{:S(2)}) async-start(), calls=%async_computation.8 | async-start | bytes 4718592 | tf_op jit(solution)/shard_map/all_gather | solution.py:34
  146.8 319.2 %reduce-scatter.5.cloned.1.call-start = ((), (), s32[]{:S(2)}) async-start(), calls=%async_computation.6 | async-start | bytes 4456448 | tf_op jit(solution)/shard_map/reduce_scatter | solution.py:48
  324.2 8.0 %copy-start.4 = (bf16[2048,1024]{1,0:T(8,128)(2,1)S(1)}, bf16[2048,1024]{1,0:T(8,128)(2,1)}, u32[]{:S(2)}) copy-start(bf16[2048,1024]{1,0:T(8,128)(2,1)} %all-gather.10.cloned.1.call-done) | copy-start | bytes 12582916
  324.3 8.0 %copy-start.5 = (bf16[2048,1024]{1,0:T(8,128)(2,1)S(1)}, bf16[2048,1024]{1,0:T(8,128)(2,1)}, u32[]{:S(2)}) copy-start(bf16[2048,1024]{1,0:T(8,128)(2,1)} %all-gather.12.cloned.1.call-done) | copy-start | bytes 12582916
  396.1 69.9 %copy-start.1 = (bf16[1024,1024]{1,0:T(8,128)(2,1)S(1)}, bf16[1024,1024]{1,0:T(8,128)(2,1)}, u32[]{:S(2)}) copy-start(bf16[1024,1024]{1,0:T(8,128)(2,1)} %param.12) | copy-start | bytes 6291460
Sparse Core Ops, SparseCore 0:
  9.7 39.7 all-gather.7
  58.0 84.6 reduce-scatter.2
  145.0 68.7 all-gather.5
  216.0 69.4 all-gather.9
  287.0 37.2 all-gather.11
  326.4 69.6 all-gather.13
  399.1 66.8 reduce-scatter.4
where the time goes:
time: 473 us
  waiting for transfers between devices  376 us (79%)
  matrix products  55.1 us (12%)
  local copies, waits for them, and re-layouts  22.8 us (5%)
  between operations  14.2 us (3%)
    reduce_scatter x1, waiting for transfers between devices, per_device(): lax.psum_scatter(lax.dot_general(cotangent, out_weight, (((1,), (1,)), ((...  84 us
    all_gather x1, waiting for transfers between devices, per_device(): lax.all_gather(gate_grad, 'col', axis=0, tiled=True)  60.2 us
    reduce_scatter x1, waiting for transfers between devices, per_device(): lax.psum_scatter((total + lax.dot_general(gate_rows, gate_weight, (((1,),...  59.7 us
    all_gather x1, waiting for transfers between devices, per_device(): lax.all_gather(branch_grad, 'col', axis=0, tiled=True)  57 us
    all_gather x1, waiting for transfers between devices, per_device(): lax.all_gather(gated, 'col', axis=0, tiled=True)  44.6 us
    all_gather x1, waiting for transfers between devices, per_device(): cotangent = lax.all_gather(out_cotangent, 'row', axis=0, tiled=True)  41.6 us
    all_gather x1, waiting for transfers between devices, per_device(): piece = lax.all_gather(saved_input, 'row', axis=0, tiled=True)  26.3 us
    unnamed x13, local copies, waits for them, and re-layouts  13 us
  transfers between devices with their start and end apart: 7, of which 7 were waited for; matrix products, arithmetic and copies ran while one was open for 16% of the time, Pallas kernels for 0%

commit v1 on v0

v1 whole, which is shorter than its diff:
```python
import jax
import jax.numpy as jnp
from jax import lax
from jax.experimental import pallas as pl
from jax.experimental.pallas import tpu as pltpu
from jax.sharding import PartitionSpec as P

MESH = pl.DeviceIdType.MESH
F32 = jnp.float32
BF16 = jnp.bfloat16
REMOTE = 64
LOCAL = 12
NT = (((1,), (1,)), ((), ()))
NN = (((1,), (0,)), ((), ()))
TN = (((0,), (0,)), ((), ()))


def dot(a, b, dims):
    return lax.dot_general(a, b, dims, preferred_element_type=F32)


def kernel(
    cot_in,
    saved_in,
    scan_in,
    gate_in,
    branch_in,
    ow_in,
    iw_in,
    ig_out,
    sg_out,
    iwg_out,
    owg_out,
    cot,
    saved,
    branch,
    gated,
    ggrad,
    ow,
    iw,
    iw_raw,
    part,
    part2,
    r_y0,
    r_half,
    r_q,
    r_x,
    r_y1,
    r2_core,
    r2_q,
    r2_x,
    r2_y,
    scan_v,
    gate_v,
    sg_v,
    ig_v,
    stage,
    owg_stage,
    ssem,
    rsem,
    lsem,
    osem,
):
    row, col = lax.axis_index("row"), lax.axis_index("col")
    yl, z, k = row // 8, (row // 2) % 4, row % 2
    x, h = col // 2, col % 2
    j = yl * 4 + z
    c = col

    def device(x=x, h=h, yl=yl, z=z, k=k):
        return ((yl * 4 + z) * 2 + k, x * 2 + h)

    xp, xm, x2 = (x + 1) % 4, (x + 3) % 4, (x + 2) % 4
    zp, zm, z2 = (z + 1) % 4, (z + 3) % 4, (z + 2) % 4
    ho, yo, ko = 1 - h, 1 - yl, 1 - k
    XP, XM, YH = device(x=xp), device(x=xm), device(h=ho)
    ZP, ZM, Z2, YL, CO = device(z=zp), device(z=zm), device(z=z2), device(yl=yo), device(k=ko)

    used = [0, 0]
    sent = []

    def send(src, dst, to):
        i = used[0]
        used[0] += 1
        copy = pltpu.make_async_remote_copy(
            src_ref=src, dst_ref=dst, send_sem=ssem.at[i], recv_sem=rsem.at[i], device_id=to, device_id_type=MESH
        )
        copy.start()
        sent.append(copy)
        return copy

    def local(src, dst):
        i = used[1]
        used[1] += 1
        copy = pltpu.make_async_copy(src, dst, lsem.at[i])
        copy.start()
        return copy

    l_cot = local(cot_in, cot.at[j, k])
    l_branch = local(branch_in, branch.at[c])
    l_scan = local(scan_in, scan_v)
    l_gate = local(gate_in, gate_v)
    l_saved = local(saved_in, saved.at[j, k])
    l_iw = local(iw_in, iw_raw)
    l_ow = local(ow_in, ow)

    barrier = pltpu.get_barrier_semaphore()
    for peer in (XP, XM, YH, ZP, ZM, Z2, YL, CO):
        pl.semaphore_signal(barrier, inc=1, device_id=peer, device_id_type=MESH)
    pl.semaphore_wait(barrier, 8)

    def row_first(buf):
        own = buf.at[j, k]
        return [send(own, own, to) for to in (YL, ZP, ZM, Z2)]

    def row_second(buf, first):
        first[0].wait_recv()
        other = buf.at[yo * 4 + z, k]
        return [send(other, other, to) for to in (ZP, ZM, Z2)]

    def row_third(buf, first, second):
        for copy in first[1:] + second:
            copy.wait_recv()
        return send(buf.at[:, k], buf.at[:, k], CO)

    def col_first(buf):
        own = buf.at[c]
        return [send(own, own, to) for to in (YH, XP, XM)]

    def col_second(buf, first):
        first[1].wait_recv()
        top = buf.at[xm * 2 + h, pl.ds(0, 128)]
        a = send(top, top, XP)
        first[2].wait_recv()
        bottom = buf.at[xp * 2 + h, pl.ds(128, 128)]
        b = send(bottom, bottom, XM)
        first[0].wait_recv()
        other = buf.at[x * 2 + ho]
        return [a, b, send(other, other, XP), send(other, other, XM)]

    def col_third(buf, second):
        out = []
        for copy, half in ((second[0], 0), (second[1], 128)):
            copy.wait_recv()
            rows = buf.at[x2 * 2 + h, pl.ds(half, 128)]
            out.append(send(rows, rows, YH))
        return out

    l_cot.wait()
    cot_a = row_first(cot)
    l_branch.wait()
    branch_a = col_first(branch)

    l_scan.wait()
    l_gate.wait()

    def gate_rows(i, carry):
        rows = pl.ds(pl.multiple_of(i * 16, 16), 16)
        v = gate_v[rows].astype(F32)
        gated[c, rows] = (scan_v[rows].astype(F32) * (v * jax.nn.sigmoid(v))).astype(BF16)
        return carry

    lax.fori_loop(0, 16, gate_rows, 0)

    cot_b = row_second(cot, cot_a)

    l_iw.wait()
    to_row = lax.broadcasted_iota(jnp.int32, (256, 256), 0)
    from_row = lax.broadcasted_iota(jnp.int32, (256, 256), 1)
    permutation = ((to_row % 16) * 16 + to_row // 16 == from_row).astype(BF16)

    def take_apart(i, carry):
        raw = iw_raw[pl.ds(pl.multiple_of(i * 256, 256), 256)]
        apart = dot(permutation, raw, NN).astype(BF16)
        rows = pl.ds(pl.multiple_of(i * 16, 16), 16)
        for g in range(16):
            iw[g % 2, rows, (g // 2) * 128 : (g // 2 + 1) * 128] = apart[g * 16 : (g + 1) * 16]
        return carry

    lax.fori_loop(0, 64, take_apart, 0)

    cot_c = row_third(cot, cot_a, cot_b)
    branch_b = col_second(branch, branch_a)
    l_saved.wait()
    saved_a = row_first(saved)
    l_ow.wait()
    cot_c.wait_recv()

    def share(chunk):
        rows = cot[chunk].reshape(256, 1024)

        def columns(n, carry):
            at = pl.multiple_of(n * 256, 256)
            part[chunk, :, pl.ds(at, 256)] = dot(rows, ow[pl.ds(at, 256)], NT).astype(BF16)
            return carry

        lax.fori_loop(0, 4, columns, 0)

    def add_to(dst, *srcs):
        def rows_of(i, carry):
            rows = pl.ds(pl.multiple_of(i * 16, 16), 16)
            total = dst[rows].astype(F32)
            for src in srcs:
                total = total + src[rows].astype(F32)
            dst[rows] = total.astype(BF16)
            return carry

        lax.fori_loop(0, dst.shape[0] // 16, rows_of, 0)

    far_o, far, next_o, prev_o = x2 * 2 + ho, x2 * 2 + h, xp * 2 + ho, xm * 2 + ho
    nxt, prev, mine_o = xp * 2 + h, xm * 2 + h, x * 2 + ho
    share(far_o)
    d0 = send(part.at[far_o], r_y0, YH)
    share(next_o)
    q0 = send(part.at[next_o], r_q.at[0], XP)
    share(prev_o)
    q1 = send(part.at[prev_o], r_q.at[1], XM)
    share(far)
    share(nxt)
    e0 = send(part.at[nxt, pl.ds(128, 128)], r_x.at[0, pl.ds(128, 128)], XP)
    share(prev)
    e1 = send(part.at[prev, pl.ds(0, 128)], r_x.at[1, pl.ds(0, 128)], XM)
    share(mine_o)
    share(c)
    saved_b = row_second(saved, saved_a)
    d0.wait_recv()
    add_to(part.at[far], r_y0)
    f0 = send(part.at[far, pl.ds(0, 128)], r_half.at[0], XP)
    f1 = send(part.at[far, pl.ds(128, 128)], r_half.at[1], XM)
    q0.wait_recv()
    q1.wait_recv()
    add_to(part.at[mine_o], r_q.at[0], r_q.at[1])
    y1 = send(part.at[mine_o], r_y1, YH)
    branch_c = col_third(branch, branch_b)
    f0.wait_recv()
    add_to(part.at[nxt, pl.ds(0, 128)], r_half.at[0])
    g0 = send(part.at[nxt, pl.ds(0, 128)], r_x.at[0, pl.ds(0, 128)], XP)
    f1.wait_recv()
    add_to(part.at[prev, pl.ds(128, 128)], r_half.at[1])
    g1 = send(part.at[prev, pl.ds(128, 128)], r_x.at[1, pl.ds(128, 128)], XM)
    saved_c = row_third(saved, saved_a, saved_b)
    for copy in (e0, e1, y1, g0, g1):
        copy.wait_recv()

    def backward_rows(i, carry):
        rows = pl.ds(pl.multiple_of(i * 16, 16), 16)
        total = part[c, rows].astype(F32) + r_x[0, rows].astype(F32)
        total = total + r_x[1, rows].astype(F32) + r_y1[rows].astype(F32)
        v = gate_v[rows].astype(F32)
        s = jax.nn.sigmoid(v)
        ggrad[c, rows] = (total * scan_v[rows].astype(F32) * s * (1.0 + v * (1.0 - s))).astype(BF16)
        sg_v[rows] = (total * (v * s)).astype(BF16)
        return carry

    lax.fori_loop(0, 16, backward_rows, 0)
    ggrad_a = col_first(ggrad)
    l_sg = local(sg_v, sg_out)

    def input_share(chunk):
        def columns(n, carry):
            at = pl.multiple_of(n * 256, 256)
            total = dot(branch[chunk], iw[0, pl.ds(at, 256)], NT)
            total = total + dot(ggrad[chunk], iw[1, pl.ds(at, 256)], NT)
            part2[chunk, :, :, pl.ds(at, 256)] = total.astype(BF16).reshape(2, 128, 256)
            return carry

        lax.fori_loop(0, 4, columns, 0)

    for copy in branch_b[2:] + branch_c:
        copy.wait_recv()
    input_share(c)
    ggrad_b = col_second(ggrad, ggrad_a)
    gated_a = col_first(gated)
    for chunk in (prev, nxt, mine_o):
        input_share(chunk)
    ggrad_c = col_third(ggrad, ggrad_b)
    input_share(far)
    ggrad_b[2].wait_recv()
    input_share(prev_o)
    ggrad_b[3].wait_recv()
    input_share(next_o)
    gated_b = col_second(gated, gated_a)
    for copy in ggrad_c:
        copy.wait_recv()
    input_share(far_o)
    saved_c.wait_recv()
    core = send(part2.at[:, ko], r2_core, CO)

    def in_weight_rows(i):
        slot = i % 2
        out = pltpu.make_async_copy(
            stage.at[slot], iwg_out.at[pl.ds(pl.multiple_of(i * 4096, 4096), 4096)], osem.at[slot]
        )

        @pl.when(i >= 2)
        def _():
            out.wait()

        features = pl.ds(pl.multiple_of(i * 256, 256), 256)
        lhs = saved[:, :, :, features].reshape(2048, 256)
        for half, buf in ((0, branch), (1, ggrad)):
            for n in range(4):
                rhs = buf[:, :, n * 256 : (n + 1) * 256].reshape(2048, 256)
                res = dot(lhs, rhs, TN)
                for t in range(2):
                    stage[slot, pl.ds(2 * (2 * n + t) + half, 256, stride=16), :] = res[:, t * 128 : (t + 1) * 128]
        out.start()

    def out_weight_rows(i):
        out = pltpu.make_async_copy(
            owg_stage, owg_out.at[pl.ds(pl.multiple_of(i * 256, 256), 256)], osem.at[2]
        )

        @pl.when(i >= 1)
        def _():
            out.wait()

        lhs = gated[:, :, pl.ds(pl.multiple_of(i * 256, 256), 256)].reshape(2048, 256)
        for n in range(4):
            rhs = cot[:, :, :, n * 256 : (n + 1) * 256].reshape(2048, 256)
            owg_stage[:, n * 256 : (n + 1) * 256] = dot(lhs, rhs, TN)
        out.start()

    def loop(low, high, body):
        def step(i, carry):
            body(i)
            return carry

        lax.fori_loop(low, high, step, 0)

    loop(0, 2, in_weight_rows)
    core.wait_recv()
    def add_cores(i, carry):
        rows = pl.ds(pl.multiple_of((i % 4) * 32, 32), 32)
        total = part2[i // 4, k, rows].astype(F32) + r2_core[i // 4, rows].astype(F32)
        part2[i // 4, k, rows] = total.astype(BF16)
        return carry

    lax.fori_loop(0, 32, add_cores, 0)
    rs_q = [send(part2.at[yo * 4 + to, k], r2_q.at[i], dev) for i, (to, dev) in enumerate(((zp, ZP), (zm, ZM), (z2, Z2)))]
    rs_x = [send(part2.at[yl * 4 + to, k], r2_x.at[i], dev) for i, (to, dev) in enumerate(((zp, ZP), (zm, ZM), (z2, Z2)))]
    loop(2, 3, in_weight_rows)
    gated_c = col_third(gated, gated_b)
    for copy in rs_q:
        copy.wait_recv()
    add_to(part2.at[yo * 4 + z, k], r2_q.at[0], r2_q.at[1], r2_q.at[2])
    rs_y = send(part2.at[yo * 4 + z, k], r2_y, YL)
    loop(3, 4, in_weight_rows)
    for copy in rs_x + [rs_y]:
        copy.wait_recv()

    def last_rows(i, carry):
        rows = pl.ds(pl.multiple_of(i * 16, 16), 16)
        total = part2[j, k, rows].astype(F32) + r2_y[rows].astype(F32)
        for t in range(3):
            total = total + r2_x[t, rows].astype(F32)
        ig_v[rows] = total.astype(BF16)
        return carry

    lax.fori_loop(0, 8, last_rows, 0)
    l_ig = local(ig_v, ig_out)
    for copy in gated_b[2:] + gated_c:
        copy.wait_recv()
    loop(0, 4, out_weight_rows)
    for slot in range(2):
        pltpu.make_async_copy(stage.at[slot], iwg_out.at[pl.ds(0, 4096)], osem.at[slot]).wait()
    pltpu.make_async_copy(owg_stage, owg_out.at[pl.ds(0, 256)], osem.at[2]).wait()
    l_sg.wait()
    l_ig.wait()
    for copy in sent:
        copy.wait_send()


def per_device(cot, saved, scan, gate, branch, ow, iw):
    iw = iw.reshape(1024, 2, 8, 128).transpose(0, 2, 1, 3).reshape(16384, 128)
    anywhere = pl.BlockSpec(memory_space=pl.ANY)
    vmem = pltpu.VMEM
    ig, sg, iwg, owg = pl.pallas_call(
        kernel,
        out_shape=[
            jax.ShapeDtypeStruct((128, 1024), BF16),
            jax.ShapeDtypeStruct((256, 1024), BF16),
            jax.ShapeDtypeStruct((16384, 128), F32),
            jax.ShapeDtypeStruct((1024, 1024), F32),
        ],
        in_specs=[anywhere] * 7,
        out_specs=[anywhere] * 4,
        scratch_shapes=[
            vmem((8, 2, 128, 1024), BF16),
            vmem((8, 2, 128, 1024), BF16),
            vmem((8, 256, 1024), BF16),
            vmem((8, 256, 1024), BF16),
            vmem((8, 256, 1024), BF16),
            vmem((1024, 1024), BF16),
            vmem((2, 1024, 1024), BF16),
            vmem((16384, 128), BF16),
            vmem((8, 256, 1024), BF16),
            vmem((8, 2, 128, 1024), BF16),
            vmem((256, 1024), BF16),
            vmem((2, 128, 1024), BF16),
            vmem((2, 256, 1024), BF16),
            vmem((2, 256, 1024), BF16),
            vmem((256, 1024), BF16),
            vmem((8, 128, 1024), BF16),
            vmem((3, 128, 1024), BF16),
            vmem((3, 128, 1024), BF16),
            vmem((128, 1024), BF16),
            vmem((256, 1024), BF16),
            vmem((256, 1024), BF16),
            vmem((256, 1024), BF16),
            vmem((128, 1024), BF16),
            vmem((2, 4096, 128), F32),
            vmem((256, 1024), F32),
            pltpu.SemaphoreType.DMA((REMOTE,)),
            pltpu.SemaphoreType.DMA((REMOTE,)),
            pltpu.SemaphoreType.DMA((LOCAL,)),
            pltpu.SemaphoreType.DMA((3,)),
        ],
        compiler_params=pltpu.CompilerParams(
            collective_id=0, has_side_effects=True, vmem_limit_bytes=60 * 1024 * 1024
        ),
        name="mixer_backward",
    )(cot, saved, scan, gate, branch, ow, iw)
    iwg = iwg.reshape(1024, 8, 2, 128).transpose(0, 2, 1, 3).reshape(1024, 2, 1024)
    return ig, sg, iwg, owg


def solution(mesh):
    return jax.shard_map(
        per_device,
        mesh=mesh,
        in_specs=(
            P("row", "col"),
            P("row", "col"),
            P("col", "row"),
            P("col", "row"),
            P("col", "row"),
            P("row", "col"),
            P("col", None, "row"),
        ),
        out_specs=(P("row", "col"), P("col", "row"), P("col", None, "row"), P("row", "col")),
        check_vma=False,
    )
```

time: 473 us -> 180 us (0.38)
  waiting for transfers between devices: 376 us -> 0 us
  Pallas kernels: 0 us -> 165 us
  matrix products: 55.1 us -> 0 us
  between operations: 14.2 us -> 0.64 us
  local copies, waits for them, and re-layouts: 22.8 us -> 13.3 us
    all_gather x5 -> x0, waiting for transfers between devices: 230 us -> none  [the longest x1 60.2 us: per_device(): lax.all_gather(gate_grad, 'col', axis=0, tiled=True)]
    pallas_call x0 -> x1, Pallas kernels: none -> 165 us  [per_device(): pl.pallas_call(kernel, out_shape=[jax.ShapeDtypeStruct((128, 1024), BF16)...]
    reduce_scatter x2 -> x0, waiting for transfers between devices: 144 us -> none  [the longest x1 84 us: per_device(): lax.psum_scatter(lax.dot_general(cotangent, out_weight, (((1,), (1,)), ((...]
    dot_general x6 -> x0, matrix products: 55.1 us -> none  [the longest x1 12.5 us: per_device(): lax.dot_general(gate_rows, gate_weight, (((1,), (1,)), ((), ())), preferr...]
    slice x1 -> x0, local copies, waits for them, and re-layouts: 9.79 us -> none  [per_device(): gate_weight = in_weight[:, 1, :]]
    unnamed x13 -> x6, local copies, waits for them, and re-layouts: 13 us -> 13.3 us
  transfers between devices with their start and end apart: 7 -> 0, of which waited for: 7 -> 0; matrix products, arithmetic and copies ran while one was open for 16% -> 0% of each run, Pallas kernels for 0% -> 0%
where the time goes in v1:
time: 180 us; the launch traced here: 179 us
  Pallas kernels  165 us (92%)
  local copies, waits for them, and re-layouts  13.3 us (7%)
    pallas_call x1, Pallas kernels, per_device(): pl.pallas_call(kernel, out_shape=[jax.ShapeDtypeStruct((128, 1024), BF16)...  165 us
    unnamed x6, local copies, waits for them, and re-layouts  13.3 us

profile of v1, /device:TPU:6, one launch (start us, length us, event | category | flops | bytes accessed | tf_op | source)
XLA Modules:
  0.0 179.1 jit_solution(12647952212632280287)
XLA Ops:
  0.6 165.2 %mixer_backward.1 = (bf16[128,1024]{1,0:T(8,128)(2,1)}, bf16[256,1024]{1,0:T(8,128)(2,1)}, f32[16384,128]{1,0:T(8,128)}, f32[1024,1024]{1,0:T(8,128)}) custom-call(bf16[128,1024]{1,0:T(8,128)(2,1)} %cot_in.1, bf16[128,1024]{1,0:T(8,128)(2,1)} %saved_in.1, bf16[256,1024]{1,0:T(8,128)(2,1)} %scan_in.1, bf16[256,1024]{1,0:T(8,128)(2,1)} %gate_in.1, ...), custom_call_target="tpu_custom_call" | custom-call | tf_op jit(solution)/shard_map/mixer_backward/pallas_call | solution.py:378
  165.8 1.7 copy.17
  167.5 1.9 %copy.18 = bf16[256,1024]{1,0:T(8,128)(2,1)} copy(bf16[256,1024]{1,0:T(8,128)(2,1)} %get-tuple-element.17) | data formatting | bytes 1048576
  169.3 0.0 copy-start
  169.3 7.8 %copy.19 = f32[1024,2,1024]{2,1,0:T(2,128)} copy(f32[1024,2,1024]{2,1,0:T(2,128)} %bitcast.10) | data formatting | bytes 16777216
  177.1 0.0 copy-done
  177.1 2.0 %copy.20 = f32[1024,1024]{1,0:T(8,128)} copy(f32[1024,1024]{1,0:T(8,128)S(1)} %copy-done) | data formatting | bytes 8388608
Async XLA Ops:
  169.3 7.8 %copy-start = (f32[1024,1024]{1,0:T(8,128)S(1)}, f32[1024,1024]{1,0:T(8,128)}, u32[]{:S(2)}) copy-start(f32[1024,1024]{1,0:T(8,128)} %get-tuple-element.19) | copy-start | bytes 12582916

commit v2 on v0

v2 whole, which is shorter than its diff:
```python
import jax
import jax.numpy as jnp
from jax import lax
from jax.experimental import pallas as pl
from jax.experimental.pallas import tpu as pltpu
from jax.sharding import PartitionSpec as P

MESH = pl.DeviceIdType.MESH
F32 = jnp.float32
BF16 = jnp.bfloat16
REMOTE = 96
VMEM_LIMIT = 40 * 1024 * 1024
LOCAL = 24
NT = (((1,), (1,)), ((), ()))
NN = (((1,), (0,)), ((), ()))
TN = (((0,), (0,)), ((), ()))


def dot(a, b, dims):
    return lax.dot_general(a, b, dims, preferred_element_type=F32)


def loop(low, high, body):
    def step(i, carry):
        body(i)
        return carry

    lax.fori_loop(low, high, step, 0)


def tokens_of(buf, chunks, columns):
    return jnp.concatenate([buf[:, chunk, :, columns].reshape(256, 256) for chunk in chunks])


def out_weight_part(gated, cot, out, i, chunks, first):
    rows = pl.ds(i * 256, 256)
    lhs = tokens_of(gated, chunks, rows)

    def columns(n):
        at = pl.ds(pl.multiple_of(n * 256, 256), 256)
        res = dot(lhs, tokens_of(cot, chunks, at), TN)
        out[rows, at] = res if first else out[rows, at] + res

    loop(0, 4, columns)


def kernel(
    cot_in,
    saved_in,
    scan_in,
    gate_in,
    branch_in,
    ow_in,
    iw_in,
    ig_v,
    sg_v,
    iwg_v,
    owg_v,
    cot,
    gated,
    saved,
    branch,
    ggrad,
    ow,
    iw,
    iw_raw,
    part,
    part2,
    r_y0,
    r_half,
    r_q,
    r_x,
    r_y1,
    r2_core,
    r2_y0,
    r2_q,
    r2_x,
    r2_y,
    scan_v,
    gate_v,
    ssem,
    rsem,
    lsem,
):
    row, col = lax.axis_index("row"), lax.axis_index("col")
    yl, z, k = row // 8, (row // 2) % 4, row % 2
    x, h = col // 2, col % 2
    j = yl * 4 + z
    c = col

    def device(x=x, h=h, yl=yl, z=z, k=k):
        return ((yl * 4 + z) * 2 + k, x * 2 + h)

    xp, xm, x2 = (x + 1) % 4, (x + 3) % 4, (x + 2) % 4
    zp, zm, z2 = (z + 1) % 4, (z + 3) % 4, (z + 2) % 4
    ho, yo, ko = 1 - h, 1 - yl, 1 - k
    XP, XM, YH = device(x=xp), device(x=xm), device(h=ho)
    ZP, ZM, Z2, YL, CO = device(z=zp), device(z=zm), device(z=z2), device(yl=yo), device(k=ko)
    far_o, far, next_o, prev_o = x2 * 2 + ho, x2 * 2 + h, xp * 2 + ho, xm * 2 + ho
    nxt, prev, mine_o = xp * 2 + h, xm * 2 + h, x * 2 + ho

    used = [0, 0]
    sent = []

    def send(src, dst, to):
        i = used[0]
        used[0] += 1
        copy = pltpu.make_async_remote_copy(
            src_ref=src, dst_ref=dst, send_sem=ssem.at[i], recv_sem=rsem.at[i], device_id=to, device_id_type=MESH
        )
        copy.start()
        sent.append(copy)
        return copy

    def local(src, dst):
        i = used[1]
        used[1] += 1
        copy = pltpu.make_async_copy(src, dst, lsem.at[i])
        copy.start()
        return copy

    def arrived(*copies):
        for copy in copies:
            copy.wait_recv()

    def done(copies):
        for copy in copies:
            copy.wait()

    def row_block(src, buf):
        return [local(src.at[pl.ds(b * 64, 64)], buf.at[b, j, pl.ds(k * 64, 64)]) for b in range(2)]

    def col_block(src, dst):
        return [
            local(src.at[pl.ds(core * 128 + b * 64, 64)], dst(b).at[pl.ds(core * 64, 64)])
            for core in range(2)
            for b in range(2)
        ]

    l_cot = row_block(cot_in, cot)
    l_branch = col_block(branch_in, lambda b: branch.at[b, c])
    l_scan = col_block(scan_in, lambda b: scan_v.at[b])
    l_gate = col_block(gate_in, lambda b: gate_v.at[b])
    l_saved = row_block(saved_in, saved)
    l_iw = [local(iw_in.at[pl.ds(p * 4096, 4096)], iw_raw.at[p]) for p in range(2)]
    l_ow = [local(ow_in, ow)]

    barrier = pltpu.get_barrier_semaphore()
    for peer in (XP, XM, YH, ZP, ZM, Z2, YL, CO):
        pl.semaphore_signal(barrier, inc=1, device_id=peer, device_id_type=MESH)
    pl.semaphore_wait(barrier, 8)

    def mine_of(buf, chip, b):
        return buf.at[:, chip, pl.ds(k * 64, 64)] if b is None else buf.at[b, chip, pl.ds(k * 64, 64)]

    def row_first(buf, b=None):
        own = mine_of(buf, j, b)
        return [send(own, own, to) for to in (YL, Z2, ZP, ZM)]

    def row_second(buf, first, b=None):
        arrived(first[0])
        other = mine_of(buf, yo * 4 + z, b)
        return [send(other, other, to) for to in ((ZP, ZM, Z2) if b is None else (ZP, ZM))]

    def row_third(buf, first, b):
        arrived(first[1])
        far_z = mine_of(buf, yl * 4 + z2, b)
        return send(far_z, far_z, YL)

    def cores(buf, b):
        block = buf.at[b, :, pl.ds(k * 64, 64)]
        return send(block, block, CO)

    def col_first(at, to=(YH, XP, XM)):
        return [send(at(c), at(c), peer) for peer in to]

    def col_second(at, first):
        arrived(first[1])
        a = send(at(prev, 0), at(prev, 0), XP)
        arrived(first[2])
        b = send(at(nxt, 1), at(nxt, 1), XM)
        arrived(first[0])
        return [a, b, send(at(mine_o), at(mine_o), XP), send(at(mine_o), at(mine_o), XM)]

    def col_third(at, second):
        out = []
        for half in range(2):
            arrived(second[half])
            out.append(send(at(far, half), at(far, half), YH))
        return out

    def col_third_x(at, second):
        arrived(second[2])
        a = send(at(prev_o, 0), at(prev_o, 0), XP)
        arrived(second[3])
        return [a, send(at(next_o, 1), at(next_o, 1), XM)]

    def whole(buf):
        def at(chunk, half=None):
            return buf.at[:, chunk] if half is None else buf.at[half, chunk]

        return at

    def batch(buf, b):
        def at(chunk, half=None):
            return buf.at[b, chunk] if half is None else buf.at[b, chunk, pl.ds(half * 64, 64)]

        return at

    to_row = lax.broadcasted_iota(jnp.int32, (256, 256), 0)
    from_row = lax.broadcasted_iota(jnp.int32, (256, 256), 1)
    permutation = ((to_row % 16) * 16 + to_row // 16 == from_row).astype(BF16)

    def take_apart(p):
        slot = p % 2
        l_iw[p].wait()

        def block(i):
            raw = iw_raw[slot, pl.ds(pl.multiple_of(i * 256, 256), 256)]
            apart = dot(permutation, raw, NN).astype(BF16)
            rows = pl.ds(pl.multiple_of(p * 256 + i * 16, 16), 16)
            for g in range(16):
                iw[g % 2, rows, (g // 2) * 128 : (g // 2 + 1) * 128] = apart[g * 16 : (g + 1) * 16]

        loop(0, 16, block)
        if p < 2:
            l_iw.append(local(iw_in.at[pl.ds((p + 2) * 4096, 4096)], iw_raw.at[slot]))

    def add_to(dst, *srcs):
        def rows_of(i):
            rows = pl.ds(pl.multiple_of(i * 16, 16), 16)
            total = dst[rows].astype(F32)
            for src in srcs:
                total = total + src[rows].astype(F32)
            dst[rows] = total.astype(BF16)

        loop(0, dst.shape[0] // 16, rows_of)

    def gate_forward():
        def rows_of(i):
            b, rows = i // 8, pl.ds(pl.multiple_of((i % 8) * 16, 16), 16)
            v = gate_v[b, rows].astype(F32)
            gated[b, c, rows] = (scan_v[b, rows].astype(F32) * (v * jax.nn.sigmoid(v))).astype(BF16)

        loop(0, 16, rows_of)

    def share(b):
        rows = cot[b].reshape(1024, 1024)

        def columns(n):
            at = pl.ds(pl.multiple_of(n * 256, 256), 256)
            part[b, :, :, at] = dot(rows, ow[at], NT).astype(BF16).reshape(8, 128, 256)

        loop(0, 4, columns)

    LOW, HIGH = pl.ds(0, 64), pl.ds(64, 64)

    def sum0(b):
        return dict(
            d=send(part.at[b, far_o], r_y0.at[b], YH),
            q=[send(part.at[b, next_o], r_q.at[b, 0], XP), send(part.at[b, prev_o], r_q.at[b, 1], XM)],
            e=[
                send(part.at[b, nxt, HIGH], r_x.at[b, 0, HIGH], XP),
                send(part.at[b, prev, LOW], r_x.at[b, 1, LOW], XM),
            ],
        )

    def sum1(b, s):
        arrived(s["d"])
        add_to(part.at[b, far], r_y0.at[b])
        s["f"] = [
            send(part.at[b, far, LOW], r_half.at[b, 0], XP),
            send(part.at[b, far, HIGH], r_half.at[b, 1], XM),
        ]

    def sum2(b, s):
        arrived(*s["q"])
        add_to(part.at[b, mine_o], r_q.at[b, 0], r_q.at[b, 1])
        s["y"] = send(part.at[b, mine_o], r_y1.at[b], YH)

    def sum3(b, s):
        arrived(s["f"][0])
        add_to(part.at[b, nxt, LOW], r_half.at[b, 0])
        g0 = send(part.at[b, nxt, LOW], r_x.at[b, 0, LOW], XP)
        arrived(s["f"][1])
        add_to(part.at[b, prev, HIGH], r_half.at[b, 1])
        g1 = send(part.at[b, prev, HIGH], r_x.at[b, 1, HIGH], XM)
        s["g"] = [g0, g1]

    def sum4(b, s):
        arrived(*s["e"], s["y"], *s["g"])

        def rows_of(i):
            rows = pl.ds(pl.multiple_of(i * 16, 16), 16)
            total = part[b, c, rows].astype(F32) + r_x[b, 0, rows].astype(F32)
            total = total + r_x[b, 1, rows].astype(F32) + r_y1[b, rows].astype(F32)
            v = gate_v[b, rows].astype(F32)
            s = jax.nn.sigmoid(v)
            ggrad[b, c, rows] = (total * scan_v[b, rows].astype(F32) * s * (1.0 + v * (1.0 - s))).astype(BF16)
            sg_v[pl.ds(pl.multiple_of((i // 4) * 128 + b * 64 + (i % 4) * 16, 16), 16)] = (total * (v * s)).astype(BF16)

        loop(0, 8, rows_of)
        return col_first(batch(ggrad, b))

    def input_share(b):
        def columns(n):
            at = pl.ds(pl.multiple_of(n * 256, 256), 256)
            total = dot(branch[b].reshape(1024, 1024), iw[0, at], NT)
            total = total + dot(ggrad[b].reshape(1024, 1024), iw[1, at], NT)
            part2[b, :, :, at] = total.astype(BF16).reshape(8, 128, 256)

        loop(0, 4, columns)

    MINE = pl.ds(pl.multiple_of(k * 64, 64), 64)
    OTHER = pl.ds(pl.multiple_of(ko * 64, 64), 64)

    def row0(b):
        return dict(c=send(part2.at[b, :, OTHER], r2_core.at[b], CO))

    def row1(b, s):
        arrived(s["c"])

        def chip(i):
            total = part2[b, i, MINE].astype(F32) + r2_core[b, i].astype(F32)
            part2[b, i, MINE] = total.astype(BF16)

        loop(0, 8, chip)
        s["d"] = send(part2.at[b, yo * 4 + z2, MINE], r2_y0.at[b], YL)
        s["q"] = [
            send(part2.at[b, yo * 4 + zp, MINE], r2_q.at[b, 0], ZP),
            send(part2.at[b, yo * 4 + zm, MINE], r2_q.at[b, 1], ZM),
        ]

    def row2(b, s):
        arrived(s["d"])
        add_to(part2.at[b, yl * 4 + z2, MINE], r2_y0.at[b])
        s["x"] = [
            send(part2.at[b, yl * 4 + z2, MINE], r2_x.at[b, 2], Z2),
            send(part2.at[b, yl * 4 + zp, MINE], r2_x.at[b, 0], ZP),
            send(part2.at[b, yl * 4 + zm, MINE], r2_x.at[b, 1], ZM),
        ]

    def row3(b, s):
        arrived(*s["q"])
        add_to(part2.at[b, yo * 4 + z, MINE], r2_q.at[b, 0], r2_q.at[b, 1])
        s["y"] = send(part2.at[b, yo * 4 + z, MINE], r2_y.at[b], YL)

    def row4(b, s):
        arrived(*s["x"], s["y"])

        def rows_of(i):
            rows = pl.ds(pl.multiple_of(i * 16, 16), 16)
            own = pl.ds(pl.multiple_of(k * 64 + i * 16, 16), 16)
            total = part2[b, j, own].astype(F32) + r2_y[b, rows].astype(F32)
            for t in range(3):
                total = total + r2_x[b, t, rows].astype(F32)
            ig_v[pl.ds(pl.multiple_of(b * 64 + i * 16, 16), 16)] = total.astype(BF16)

        loop(0, 4, rows_of)

    def in_weight_rows(half, i):
        buf = (branch, ggrad)[half]
        lhs = saved[:, :, :, i * 256 : (i + 1) * 256].reshape(2048, 256)

        def columns(n):
            at = pl.ds(pl.multiple_of(n * 256, 256), 256)
            res = dot(lhs, buf[:, :, :, at].reshape(2048, 256), TN)
            for t in range(2):
                iwg_v[pl.ds(i * 4096 + 4 * n + 2 * t + half, 256, stride=16), :] = res[:, t * 128 : (t + 1) * 128]

        loop(0, 4, columns)

    def out_weight_rows(i):
        out_weight_part(gated, cot, owg_v, i, (c, prev, nxt, mine_o, far), True)

    done(l_cot)
    cot1 = row_first(cot)
    done(l_branch)
    branch1 = col_first(whole(branch))
    done(l_scan + l_gate)
    gate_forward()
    cot2 = row_second(cot, cot1)
    take_apart(0)
    branch2 = col_second(whole(branch), branch1)
    branch3 = col_third(whole(branch), branch2)
    arrived(*cot1[1:], *cot2)
    cot4 = cores(cot, 0)
    done(l_saved)
    saved1 = row_first(saved)
    done(l_ow)
    arrived(cot4)
    cot5 = cores(cot, 1)
    share(0)
    sa = sum0(0)
    arrived(cot5)
    share(1)
    sum1(0, sa)
    sb = sum0(1)
    take_apart(1)
    saved2 = row_second(saved, saved1)
    sum2(0, sa)
    sum3(0, sa)
    sum1(1, sb)
    sum2(1, sb)
    ga1 = sum4(0, sa)
    sum3(1, sb)
    take_apart(2)
    ga2 = col_second(batch(ggrad, 0), ga1)
    gb1 = sum4(1, sb)
    arrived(*saved1[1:], *saved2)
    saved4 = cores(saved, 0)
    take_apart(3)
    arrived(saved4)
    saved5 = cores(saved, 1)
    ga3 = col_third(batch(ggrad, 0), ga2)
    arrived(saved5)
    arrived(*branch2[2:], *branch3)
    in_weight_rows(0, 0)
    gb2 = col_second(batch(ggrad, 1), gb1)
    gated1 = col_first(whole(gated), (XP, XM))
    in_weight_rows(0, 1)
    arrived(*ga2[2:], *ga3)
    gb3 = col_third(batch(ggrad, 1), gb2)
    gated1 = col_first(whole(gated), (YH,)) + gated1
    input_share(0)
    ra = row0(0)
    in_weight_rows(0, 2)
    row1(0, ra)
    in_weight_rows(0, 3)
    row2(0, ra)
    arrived(*gb2[2:], *gb3)
    input_share(1)
    rb = row0(1)
    row3(0, ra)
    gated2 = col_second(whole(gated), gated1)
    row1(1, rb)
    in_weight_rows(1, 0)
    row2(1, rb)
    in_weight_rows(1, 1)
    row3(1, rb)
    in_weight_rows(1, 2)
    row4(0, ra)
    in_weight_rows(1, 3)
    gated3 = col_third_x(whole(gated), gated2)
    row4(1, rb)
    arrived(*gated2[:2])
    for i in range(4):
        out_weight_rows(i)
    arrived(*gated3)
    for copy in sent:
        copy.wait_send()


def write_out(ig, sg, iwg, owg, cot, gated, ig_out, sg_out, iwg_out, owg_out, sem):
    def store(i, src, dst):
        copy = pltpu.make_async_copy(src, dst, sem.at[i])
        copy.start()
        return copy

    copies = [store(0, iwg, iwg_out), store(1, sg, sg_out), store(2, ig, ig_out)]
    col = lax.axis_index("col")
    x, ho = col // 2, 1 - col % 2
    chunks = [(x + step) % 4 * 2 + ho for step in (1, 2, 3)]
    for i in range(4):
        out_weight_part(gated, cot, owg, i, chunks, False)
        rows = pl.ds(i * 256, 256)
        copies.append(store(3 + i, owg.at[rows], owg_out.at[rows]))
    for copy in copies:
        copy.wait()


def per_device(cot, saved, scan, gate, branch, ow, iw):
    iw = iw.reshape(1024, 2, 8, 128).transpose(0, 2, 1, 3).reshape(16384, 128)
    anywhere = pl.BlockSpec(memory_space=pl.ANY)
    tokens = pltpu.VMEM((2, 8, 128, 1024), BF16)

    def blocks(*shape):
        return pltpu.VMEM((*shape, 1024), BF16)

    results = ((128, 1024), BF16), ((256, 1024), BF16), ((16384, 128), F32), ((1024, 1024), F32)
    passed = (((2, 8, 128, 1024), BF16),) * 2
    held = pl.pallas_call(
        kernel,
        out_shape=[pltpu.VMEM(shape, dtype) for shape, dtype in results + passed],
        in_specs=[anywhere] * 7,
        out_specs=[pl.BlockSpec(memory_space=pltpu.VMEM)] * 6,
        scratch_shapes=[
            tokens,
            tokens,
            tokens,
            blocks(1024),
            blocks(2, 1024),
            pltpu.VMEM((2, 4096, 128), BF16),
            tokens,
            tokens,
            blocks(2, 128),
            blocks(2, 2, 64),
            blocks(2, 2, 128),
            blocks(2, 2, 128),
            blocks(2, 128),
            blocks(2, 8, 64),
            blocks(2, 64),
            blocks(2, 2, 64),
            blocks(2, 3, 64),
            blocks(2, 64),
            blocks(2, 128),
            blocks(2, 128),
            pltpu.SemaphoreType.DMA((REMOTE,)),
            pltpu.SemaphoreType.DMA((REMOTE,)),
            pltpu.SemaphoreType.DMA((LOCAL,)),
        ],
        compiler_params=pltpu.CompilerParams(
            collective_id=0, has_side_effects=True, vmem_limit_bytes=VMEM_LIMIT
        ),
        name="mixer_backward",
    )(cot, saved, scan, gate, branch, ow, iw)
    ig, sg, iwg, owg = pl.pallas_call(
        write_out,
        out_shape=[jax.ShapeDtypeStruct(shape, dtype) for shape, dtype in results],
        in_specs=[pl.BlockSpec(memory_space=pltpu.VMEM)] * 6,
        out_specs=[anywhere] * 4,
        scratch_shapes=[pltpu.SemaphoreType.DMA((7,))],
        compiler_params=pltpu.CompilerParams(vmem_limit_bytes=4 * 1024 * 1024),
        name="write_out",
    )(*[pltpu.with_memory_space_constraint(array, pltpu.VMEM) for array in held])
    iwg = iwg.reshape(1024, 8, 2, 128).transpose(0, 2, 1, 3).reshape(1024, 2, 1024)
    return ig, sg, iwg, owg


def solution(mesh):
    return jax.shard_map(
        per_device,
        mesh=mesh,
        in_specs=(
            P("row", "col"),
            P("row", "col"),
            P("col", "row"),
            P("col", "row"),
            P("col", "row"),
            P("row", "col"),
            P("col", None, "row"),
        ),
        out_specs=(P("row", "col"), P("col", "row"), P("col", None, "row"), P("row", "col")),
        check_vma=False,
    )
```

time: 473 us -> 150 us (0.32)
  waiting for transfers between devices: 376 us -> 0 us
  Pallas kernels: 0 us -> 148 us
  matrix products: 55.1 us -> 0 us
  local copies, waits for them, and re-layouts: 22.8 us -> 0 us
  between operations: 14.2 us -> 0.64 us
    all_gather x5 -> x0, waiting for transfers between devices: 230 us -> none  [the longest x1 60.2 us: per_device(): lax.all_gather(gate_grad, 'col', axis=0, tiled=True)]
    pallas_call x0 -> x2, Pallas kernels: none -> 148 us  [the longest x1 141 us: per_device(): pl.pallas_call(kernel, out_shape=[pltpu.VMEM(shape, dtype) for shape, dty...]
    reduce_scatter x2 -> x0, waiting for transfers between devices: 144 us -> none  [the longest x1 84 us: per_device(): lax.psum_scatter(lax.dot_general(cotangent, out_weight, (((1,), (1,)), ((...]
    dot_general x6 -> x0, matrix products: 55.1 us -> none  [the longest x1 12.5 us: per_device(): lax.dot_general(gate_rows, gate_weight, (((1,), (1,)), ((), ())), preferr...]
    unnamed x13 -> x0, local copies, waits for them, and re-layouts: 13 us -> none
    slice x1 -> x0, local copies, waits for them, and re-layouts: 9.79 us -> none  [per_device(): gate_weight = in_weight[:, 1, :]]
  transfers between devices with their start and end apart: 7 -> 0, of which waited for: 7 -> 0; matrix products, arithmetic and copies ran while one was open for 16% -> 0% of each run, Pallas kernels for 0% -> 0%
where the time goes in v2:
time: 150 us; the launch traced here: 148 us
  Pallas kernels  148 us (99%)
    pallas_call x1, Pallas kernels, per_device(): pl.pallas_call(kernel, out_shape=[pltpu.VMEM(shape, dtype) for shape, dty...  141 us
    pallas_call x1, Pallas kernels, per_device(): pl.pallas_call(write_out, out_shape=[jax.ShapeDtypeStruct(shape, dtype) f...  6.42 us

profile of v2, /device:TPU:6, one launch (start us, length us, event | category | flops | bytes accessed | tf_op | source)
XLA Modules:
  0.0 148.2 jit_solution(516772327962747793)
XLA Ops:
  0.6 141.1 %mixer_backward.1 = (bf16[128,1024]{1,0:T(8,128)(2,1)S(1)}, bf16[256,1024]{1,0:T(8,128)(2,1)S(1)}, f32[16384,128]{1,0:T(8,128)S(1)}, f32[1024,1024]{1,0:T(8,128)...) custom-call(bf16[128,1024]{1,0:T(8,128)(2,1)} %cot_in.1, bf16[128,1024]{1,0:T(8,128)(2,1)} %saved_in.1, ...), custom_call_target="tpu_custom_call" | custom-call | tf_op jit(solution)/shard_map/mixer_backward/pallas_call | solution.py:482
  141.8 6.4 %write_out.1 = (bf16[128,1024]{1,0:T(8,128)(2,1)}, bf16[256,1024]{1,0:T(8,128)(2,1)}, f32[16384,128]{1,0:T(8,128)}, f32[1024,1024]{1,0:T(8,128)}) custom-call(bf16[128,1024]{1,0:T(8,128)(2,1)S(1)} %get-tuple-element.14.ig, bf16[256,1024]{1,0:T(8,128)(2,1)S(1)} %get-tuple-element.15.sg, f32[16384,128]{1,0:T(8,128)S(1)} %get-tuple-element.16.iwg, ...), custom_call_target="tpu_custom_call" | custom-call | tf_op jit(solution)/shard_map/write_out/pallas_call | solution.py:517

commit v3 on v2

--- a/solution.py
+++ b/solution.py
@@ -29,19 +29,13 @@
 
 
 def tokens_of(buf, chunks, columns):
-    return jnp.concatenate([buf[:, chunk, :, columns].reshape(256, 256) for chunk in chunks])
+    return jnp.concatenate([buf[:, chunk, :, columns].reshape(256, columns.size) for chunk in chunks])
 
 
 def out_weight_part(gated, cot, out, i, chunks, first):
     rows = pl.ds(i * 256, 256)
-    lhs = tokens_of(gated, chunks, rows)
-
-    def columns(n):
-        at = pl.ds(pl.multiple_of(n * 256, 256), 256)
-        res = dot(lhs, tokens_of(cot, chunks, at), TN)
-        out[rows, at] = res if first else out[rows, at] + res
-
-    loop(0, 4, columns)
+    res = dot(tokens_of(gated, chunks, rows), tokens_of(cot, chunks, pl.ds(0, 1024)), TN)
+    out[rows] = res if first else out[rows] + res
 
 
 def kernel(
@@ -72,7 +66,6 @@
     r_x,
     r_y1,
     r2_core,
-    r2_y0,
     r2_q,
     r2_x,
     r2_y,
@@ -174,26 +167,29 @@
     def col_first(at, to=(YH, XP, XM)):
         return [send(at(c), at(c), peer) for peer in to]
 
-    def col_second(at, first):
+    def col_halves(at, first):
         arrived(first[1])
         a = send(at(prev, 0), at(prev, 0), XP)
         arrived(first[2])
-        b = send(at(nxt, 1), at(nxt, 1), XM)
+        return [a, send(at(nxt, 1), at(nxt, 1), XM)]
+
+    def col_other(at, first):
         arrived(first[0])
-        return [a, b, send(at(mine_o), at(mine_o), XP), send(at(mine_o), at(mine_o), XM)]
-
-    def col_third(at, second):
+        return [send(at(mine_o), at(mine_o), to) for to in (XP, XM)]
+
+    def col_second(at, first):
+        return col_halves(at, first) + col_other(at, first)
+
+    def col_first_split(at):
+        ways = ((0, XP), (1, XM), (1, XP), (0, XM))
+        return [send(at(c, half), at(c, half), peer) for half, peer in ways]
+
+    def col_third(at, second, halves=(0, 1)):
         out = []
-        for half in range(2):
+        for half in halves:
             arrived(second[half])
             out.append(send(at(far, half), at(far, half), YH))
         return out
-
-    def col_third_x(at, second):
-        arrived(second[2])
-        a = send(at(prev_o, 0), at(prev_o, 0), XP)
-        arrived(second[3])
-        return [a, send(at(next_o, 1), at(next_o, 1), XM)]
 
     def whole(buf):
         def at(chunk, half=None):
@@ -325,24 +321,13 @@
             part2[b, i, MINE] = total.astype(BF16)
 
         loop(0, 8, chip)
-        s["d"] = send(part2.at[b, yo * 4 + z2, MINE], r2_y0.at[b], YL)
-        s["q"] = [
-            send(part2.at[b, yo * 4 + zp, MINE], r2_q.at[b, 0], ZP),
-            send(part2.at[b, yo * 4 + zm, MINE], r2_q.at[b, 1], ZM),
-        ]
-
-    def row2(b, s):
-        arrived(s["d"])
-        add_to(part2.at[b, yl * 4 + z2, MINE], r2_y0.at[b])
-        s["x"] = [
-            send(part2.at[b, yl * 4 + z2, MINE], r2_x.at[b, 2], Z2),
-            send(part2.at[b, yl * 4 + zp, MINE], r2_x.at[b, 0], ZP),
-            send(part2.at[b, yl * 4 + zm, MINE], r2_x.at[b, 1], ZM),
-        ]
+        ways = ((zp, ZP), (zm, ZM), (z2, Z2))
+        s["q"] = [send(part2.at[b, yo * 4 + to, MINE], r2_q.at[b, i], dev) for i, (to, dev) in enumerate(ways)]
+        s["x"] = [send(part2.at[b, yl * 4 + to, MINE], r2_x.at[b, i], dev) for i, (to, dev) in enumerate(ways)]
 
     def row3(b, s):
         arrived(*s["q"])
-        add_to(part2.at[b, yo * 4 + z, MINE], r2_q.at[b, 0], r2_q.at[b, 1])
+        add_to(part2.at[b, yo * 4 + z, MINE], r2_q.at[b, 0], r2_q.at[b, 1], r2_q.at[b, 2])
         s["y"] = send(part2.at[b, yo * 4 + z, MINE], r2_y.at[b], YL)
 
     def row4(b, s):
@@ -362,13 +347,9 @@
         buf = (branch, ggrad)[half]
         lhs = saved[:, :, :, i * 256 : (i + 1) * 256].reshape(2048, 256)
 
-        def columns(n):
-            at = pl.ds(pl.multiple_of(n * 256, 256), 256)
-            res = dot(lhs, buf[:, :, :, at].reshape(2048, 256), TN)
-            for t in range(2):
-                iwg_v[pl.ds(i * 4096 + 4 * n + 2 * t + half, 256, stride=16), :] = res[:, t * 128 : (t + 1) * 128]
-
-        loop(0, 4, columns)
+        res = dot(lhs, buf[...].reshape(2048, 1024), TN)
+        for t in range(8):
+            iwg_v[pl.ds(i * 4096 + 2 * t + half, 256, stride=16), :] = res[:, t * 128 : (t + 1) * 128]
 
     def out_weight_rows(i):
         out_weight_part(gated, cot, owg_v, i, (c, prev, nxt, mine_o, far), True)
@@ -382,11 +363,11 @@
     cot2 = row_second(cot, cot1)
     take_apart(0)
     branch2 = col_second(whole(branch), branch1)
-    branch3 = col_third(whole(branch), branch2)
+    done(l_saved)
+    saved1 = row_first(saved)
+    branch3 = col_third(whole(branch), branch2, (0,))
     arrived(*cot1[1:], *cot2)
     cot4 = cores(cot, 0)
-    done(l_saved)
-    saved1 = row_first(saved)
     done(l_ow)
     arrived(cot4)
     cot5 = cores(cot, 1)
@@ -403,6 +384,7 @@
     sum1(1, sb)
     sum2(1, sb)
     ga1 = sum4(0, sa)
+    branch3 += col_third(whole(branch), branch2, (1,))
     sum3(1, sb)
     take_apart(2)
     ga2 = col_second(batch(ggrad, 0), ga1)
@@ -410,43 +392,43 @@
     arrived(*saved1[1:], *saved2)
     saved4 = cores(saved, 0)
     take_apart(3)
+    ga3 = col_third(batch(ggrad, 0), ga2)
     arrived(saved4)
     saved5 = cores(saved, 1)
-    ga3 = col_third(batch(ggrad, 0), ga2)
+    arrived(*branch2[2:], *branch3)
     arrived(saved5)
-    arrived(*branch2[2:], *branch3)
     in_weight_rows(0, 0)
+    in_weight_rows(0, 1)
     gb2 = col_second(batch(ggrad, 1), gb1)
-    gated1 = col_first(whole(gated), (XP, XM))
-    in_weight_rows(0, 1)
-    arrived(*ga2[2:], *ga3)
+    gated1 = col_first_split(whole(gated))
+    in_weight_rows(0, 2)
     gb3 = col_third(batch(ggrad, 1), gb2)
     gated1 = col_first(whole(gated), (YH,)) + gated1
+    arrived(*ga2[2:], *ga3)
     input_share(0)
     ra = row0(0)
-    in_weight_rows(0, 2)
+    in_weight_rows(0, 3)
     row1(0, ra)
-    in_weight_rows(0, 3)
-    row2(0, ra)
     arrived(*gb2[2:], *gb3)
     input_share(1)
     rb = row0(1)
+    gated2 = col_halves(whole(gated), gated1)
     row3(0, ra)
-    gated2 = col_second(whole(gated), gated1)
+    in_weight_rows(1, 0)
+    gated2 += col_other(whole(gated), gated1)
     row1(1, rb)
-    in_weight_rows(1, 0)
-    row2(1, rb)
     in_weight_rows(1, 1)
-    row3(1, rb)
+    gated3 = col_third(whole(gated), gated2, (0,))
     in_weight_rows(1, 2)
     row4(0, ra)
     in_weight_rows(1, 3)
-    gated3 = col_third_x(whole(gated), gated2)
-    row4(1, rb)
-    arrived(*gated2[:2])
+    row3(1, rb)
+    gated3 += col_third(whole(gated), gated2, (1,))
+    arrived(*gated1[3:])
     for i in range(4):
         out_weight_rows(i)
-    arrived(*gated3)
+    row4(1, rb)
+    arrived(*gated2[2:], *gated3)
     for copy in sent:
         copy.wait_send()
 
@@ -499,8 +481,7 @@
             blocks(2, 2, 128),
             blocks(2, 128),
             blocks(2, 8, 64),
-            blocks(2, 64),
-            blocks(2, 2, 64),
+            blocks(2, 3, 64),
             blocks(2, 3, 64),
             blocks(2, 64),
             blocks(2, 128),

time: 150 us -> 138 us (0.920); the launches traced: 148 us -> 138 us
  Pallas kernels: 148 us -> 137 us
    pallas_call x1, Pallas kernels: 141 us -> 132 us  [per_device(): pl.pallas_call(kernel, out_shape=[pltpu.VMEM(shape, dtype) for shape, dty...]
where the time goes in v3:
time: 138 us
  Pallas kernels  137 us (99%)
    pallas_call x1, Pallas kernels, per_device(): pl.pallas_call(kernel, out_shape=[pltpu.VMEM(shape, dtype) for shape, dty...  132 us
    pallas_call x1, Pallas kernels, per_device(): pl.pallas_call(write_out, out_shape=[jax.ShapeDtypeStruct(shape, dtype) f...  5 us

profile of v3, /device:TPU:6, one launch (start us, length us, event | category | flops | bytes accessed | tf_op | source)
XLA Modules:
  0.0 137.8 jit_solution(12421453088936398717)
XLA Ops:
  0.6 132.0 %mixer_backward.1 = (bf16[128,1024]{1,0:T(8,128)(2,1)S(1)}, bf16[256,1024]{1,0:T(8,128)(2,1)S(1)}, f32[16384,128]{1,0:T(8,128)S(1)}, f32[1024,1024]{1,0:T(8,128)...) custom-call(bf16[128,1024]{1,0:T(8,128)(2,1)} %cot_in.1, bf16[128,1024]{1,0:T(8,128)(2,1)} %saved_in.1, ...), custom_call_target="tpu_custom_call" | custom-call | tf_op jit(solution)/shard_map/mixer_backward/pallas_call | solution.py:464
  132.7 5.0 %write_out.1 = (bf16[128,1024]{1,0:T(8,128)(2,1)}, bf16[256,1024]{1,0:T(8,128)(2,1)}, f32[16384,128]{1,0:T(8,128)}, f32[1024,1024]{1,0:T(8,128)}) custom-call(bf16[128,1024]{1,0:T(8,128)(2,1)S(1)} %get-tuple-element.14.ig, bf16[256,1024]{1,0:T(8,128)(2,1)S(1)} %get-tuple-element.15.sg, f32[16384,128]{1,0:T(8,128)S(1)} %get-tuple-element.16.iwg, ...), custom_call_target="tpu_custom_call" | custom-call | tf_op jit(solution)/shard_map/write_out/pallas_call | solution.py:498

commit v4 on v3

--- a/solution.py
+++ b/solution.py
@@ -180,8 +180,7 @@
     def col_second(at, first):
         return col_halves(at, first) + col_other(at, first)
 
-    def col_first_split(at):
-        ways = ((0, XP), (1, XM), (1, XP), (0, XM))
+    def col_first_split(at, ways):
         return [send(at(c, half), at(c, half), peer) for half, peer in ways]
 
     def col_third(at, second, halves=(0, 1)):
@@ -306,6 +305,21 @@
             part2[b, :, :, at] = total.astype(BF16).reshape(8, 128, 256)
 
         loop(0, 4, columns)
+
+    def input_share_branch(b):
+        def columns(n):
+            at = pl.ds(pl.multiple_of(n * 256, 256), 256)
+            owg_v[:, at] = dot(branch[b].reshape(1024, 1024), iw[0, at], NT)
+
+        loop(0, 4, columns)
+
+    def input_share_gate(b, low, high):
+        def columns(n):
+            at = pl.ds(pl.multiple_of(n * 256, 256), 256)
+            total = owg_v[:, at] + dot(ggrad[b].reshape(1024, 1024), iw[1, at], NT)
+            part2[b, :, :, at] = total.astype(BF16).reshape(8, 128, 256)
+
+        loop(low, high, columns)
 
     MINE = pl.ds(pl.multiple_of(k * 64, 64), 64)
     OTHER = pl.ds(pl.multiple_of(ko * 64, 64), 64)
@@ -389,41 +403,44 @@
     take_apart(2)
     ga2 = col_second(batch(ggrad, 0), ga1)
     gb1 = sum4(1, sb)
+    gated1 = col_first_split(whole(gated), ((0, XP), (1, XM)))
     arrived(*saved1[1:], *saved2)
     saved4 = cores(saved, 0)
     take_apart(3)
     ga3 = col_third(batch(ggrad, 0), ga2)
+    gated1 = col_first(whole(gated), (YH,)) + gated1
     arrived(saved4)
     saved5 = cores(saved, 1)
     arrived(*branch2[2:], *branch3)
+    input_share_branch(1)
     arrived(saved5)
     in_weight_rows(0, 0)
     in_weight_rows(0, 1)
     gb2 = col_second(batch(ggrad, 1), gb1)
-    gated1 = col_first_split(whole(gated))
     in_weight_rows(0, 2)
-    gb3 = col_third(batch(ggrad, 1), gb2)
-    gated1 = col_first(whole(gated), (YH,)) + gated1
+    in_weight_rows(0, 3)
     arrived(*ga2[2:], *ga3)
     input_share(0)
     ra = row0(0)
-    in_weight_rows(0, 3)
+    gated2 = col_halves(whole(gated), gated1)
+    gated1 += col_first_split(whole(gated), ((1, XP), (0, XM)))
+    gb3 = col_third(batch(ggrad, 1), gb2)
     row1(0, ra)
+    gated2 += col_other(whole(gated), gated1)
     arrived(*gb2[2:], *gb3)
-    input_share(1)
+    input_share_gate(1, 0, 3)
+    gated3 = col_third(whole(gated), gated2, (0,))
+    input_share_gate(1, 3, 4)
     rb = row0(1)
-    gated2 = col_halves(whole(gated), gated1)
     row3(0, ra)
     in_weight_rows(1, 0)
-    gated2 += col_other(whole(gated), gated1)
+    gated3 += col_third(whole(gated), gated2, (1,))
     row1(1, rb)
     in_weight_rows(1, 1)
-    gated3 = col_third(whole(gated), gated2, (0,))
     in_weight_rows(1, 2)
+    in_weight_rows(1, 3)
     row4(0, ra)
-    in_weight_rows(1, 3)
     row3(1, rb)
-    gated3 += col_third(whole(gated), gated2, (1,))
     arrived(*gated1[3:])
     for i in range(4):
         out_weight_rows(i)

time: 138 us -> 133 us (0.964); the launches traced: 138 us -> 131 us
  Pallas kernels: 137 us -> 130 us
    pallas_call x1, Pallas kernels: 132 us -> 125 us  [per_device(): pl.pallas_call(kernel, out_shape=[pltpu.VMEM(shape, dtype) for shape, dty...]
where the time goes in v4:
time: 133 us; the launch traced here: 131 us
  Pallas kernels  130 us (98%)
    pallas_call x1, Pallas kernels, per_device(): pl.pallas_call(kernel, out_shape=[pltpu.VMEM(shape, dtype) for shape, dty...  125 us
    pallas_call x1, Pallas kernels, per_device(): pl.pallas_call(write_out, out_shape=[jax.ShapeDtypeStruct(shape, dtype) f...  5 us

profile of v4, /device:TPU:6, one launch (start us, length us, event | category | flops | bytes accessed | tf_op | source)
XLA Modules:
  0.0 130.9 jit_solution(930934723815696218)
XLA Ops:
  0.6 125.1 %mixer_backward.1 = (bf16[128,1024]{1,0:T(8,128)(2,1)S(1)}, bf16[256,1024]{1,0:T(8,128)(2,1)S(1)}, f32[16384,128]{1,0:T(8,128)S(1)}, f32[1024,1024]{1,0:T(8,128)...) custom-call(bf16[128,1024]{1,0:T(8,128)(2,1)} %cot_in.1, bf16[128,1024]{1,0:T(8,128)(2,1)} %saved_in.1, ...), custom_call_target="tpu_custom_call" | custom-call | tf_op jit(solution)/shard_map/mixer_backward/pallas_call | solution.py:481
  125.7 5.0 %write_out.1 = (bf16[128,1024]{1,0:T(8,128)(2,1)}, bf16[256,1024]{1,0:T(8,128)(2,1)}, f32[16384,128]{1,0:T(8,128)}, f32[1024,1024]{1,0:T(8,128)}) custom-call(bf16[128,1024]{1,0:T(8,128)(2,1)S(1)} %get-tuple-element.14.ig, bf16[256,1024]{1,0:T(8,128)(2,1)S(1)} %get-tuple-element.15.sg, f32[16384,128]{1,0:T(8,128)S(1)} %get-tuple-element.16.iwg, ...), custom_call_target="tpu_custom_call" | custom-call | tf_op jit(solution)/shard_map/write_out/pallas_call | solution.py:515

commit v5 on v4

--- a/solution.py
+++ b/solution.py
@@ -306,23 +306,28 @@
 
         loop(0, 4, columns)
 
+    MINE = pl.ds(pl.multiple_of(k * 64, 64), 64)
+    OTHER = pl.ds(pl.multiple_of(ko * 64, 64), 64)
+    HALVES = ((OTHER, pl.ds(0, 512)), (MINE, pl.ds(512, 512)))
+
     def input_share_branch(b):
+        for tokens, rows in HALVES:
+
+            def columns(n):
+                at = pl.ds(pl.multiple_of(n * 256, 256), 256)
+                owg_v[rows, at] = dot(branch[b, :, tokens].reshape(512, 1024), iw[0, at], NT)
+
+            loop(0, 4, columns)
+
+    def input_share_gate(b, half, low=0, high=4):
+        tokens, rows = HALVES[half]
+
         def columns(n):
             at = pl.ds(pl.multiple_of(n * 256, 256), 256)
-            owg_v[:, at] = dot(branch[b].reshape(1024, 1024), iw[0, at], NT)
-
-        loop(0, 4, columns)
-
-    def input_share_gate(b, low, high):
-        def columns(n):
-            at = pl.ds(pl.multiple_of(n * 256, 256), 256)
-            total = owg_v[:, at] + dot(ggrad[b].reshape(1024, 1024), iw[1, at], NT)
-            part2[b, :, :, at] = total.astype(BF16).reshape(8, 128, 256)
+            total = owg_v[rows, at] + dot(ggrad[b, :, tokens].reshape(512, 1024), iw[1, at], NT)
+            part2[b, :, tokens, at] = total.astype(BF16).reshape(8, 64, 256)
 
         loop(low, high, columns)
-
-    MINE = pl.ds(pl.multiple_of(k * 64, 64), 64)
-    OTHER = pl.ds(pl.multiple_of(ko * 64, 64), 64)
 
     def row0(b):
         return dict(c=send(part2.at[b, :, OTHER], r2_core.at[b], CO))
@@ -335,7 +340,7 @@
             part2[b, i, MINE] = total.astype(BF16)
 
         loop(0, 8, chip)
-        ways = ((zp, ZP), (zm, ZM), (z2, Z2))
+        ways = ((z2, Z2), (zp, ZP), (zm, ZM))
         s["q"] = [send(part2.at[b, yo * 4 + to, MINE], r2_q.at[b, i], dev) for i, (to, dev) in enumerate(ways)]
         s["x"] = [send(part2.at[b, yl * 4 + to, MINE], r2_x.at[b, i], dev) for i, (to, dev) in enumerate(ways)]
 
@@ -417,8 +422,6 @@
     in_weight_rows(0, 0)
     in_weight_rows(0, 1)
     gb2 = col_second(batch(ggrad, 1), gb1)
-    in_weight_rows(0, 2)
-    in_weight_rows(0, 3)
     arrived(*ga2[2:], *ga3)
     input_share(0)
     ra = row0(0)
@@ -426,19 +429,20 @@
     gated1 += col_first_split(whole(gated), ((1, XP), (0, XM)))
     gb3 = col_third(batch(ggrad, 1), gb2)
     row1(0, ra)
+    in_weight_rows(0, 2)
     gated2 += col_other(whole(gated), gated1)
+    in_weight_rows(0, 3)
     arrived(*gb2[2:], *gb3)
-    input_share_gate(1, 0, 3)
-    gated3 = col_third(whole(gated), gated2, (0,))
-    input_share_gate(1, 3, 4)
+    input_share_gate(1, 0)
     rb = row0(1)
     row3(0, ra)
-    in_weight_rows(1, 0)
+    input_share_gate(1, 1, 0, 2)
+    gated3 = col_third(whole(gated), gated2, (0,))
+    input_share_gate(1, 1, 2, 4)
+    row1(1, rb)
     gated3 += col_third(whole(gated), gated2, (1,))
-    row1(1, rb)
-    in_weight_rows(1, 1)
-    in_weight_rows(1, 2)
-    in_weight_rows(1, 3)
+    for i in range(4):
+        in_weight_rows(1, i)
     row4(0, ra)
     row3(1, rb)
     arrived(*gated1[3:])
@@ -456,14 +460,16 @@
         copy.start()
         return copy
 
-    copies = [store(0, iwg, iwg_out), store(1, sg, sg_out), store(2, ig, ig_out)]
+    quarters = [pl.ds(i * 4096, 4096) for i in range(4)]
+    copies = [store(6 + i, iwg.at[rows], iwg_out.at[rows]) for i, rows in enumerate(quarters)]
+    copies += [store(0, sg, sg_out), store(1, ig, ig_out)]
     col = lax.axis_index("col")
     x, ho = col // 2, 1 - col % 2
     chunks = [(x + step) % 4 * 2 + ho for step in (1, 2, 3)]
     for i in range(4):
         out_weight_part(gated, cot, owg, i, chunks, False)
         rows = pl.ds(i * 256, 256)
-        copies.append(store(3 + i, owg.at[rows], owg_out.at[rows]))
+        copies.append(store(2 + i, owg.at[rows], owg_out.at[rows]))
     for copy in copies:
         copy.wait()
 
@@ -517,7 +523,7 @@
         out_shape=[jax.ShapeDtypeStruct(shape, dtype) for shape, dtype in results],
         in_specs=[pl.BlockSpec(memory_space=pltpu.VMEM)] * 6,
         out_specs=[anywhere] * 4,
-        scratch_shapes=[pltpu.SemaphoreType.DMA((7,))],
+        scratch_shapes=[pltpu.SemaphoreType.DMA((10,))],
         compiler_params=pltpu.CompilerParams(vmem_limit_bytes=4 * 1024 * 1024),
         name="write_out",
     )(*[pltpu.with_memory_space_constraint(array, pltpu.VMEM) for array in held])

time: 133 us -> 132 us (level)
  no operation moved by 1% of the time
where the time goes in v5:
time: 132 us; the launch traced here: 130 us
  Pallas kernels  129 us (98%)
    pallas_call x1, Pallas kernels, per_device(): pl.pallas_call(kernel, out_shape=[pltpu.VMEM(shape, dtype) for shape, dty...  124 us
    pallas_call x1, Pallas kernels, per_device(): pl.pallas_call(write_out, out_shape=[jax.ShapeDtypeStruct(shape, dtype) f...  4.91 us

profile of v5, /device:TPU:6, one launch (start us, length us, event | category | flops | bytes accessed | tf_op | source)
XLA Modules:
  0.0 130.0 jit_solution(3816451476762910505)
XLA Ops:
  0.6 124.3 %mixer_backward.1 = (bf16[128,1024]{1,0:T(8,128)(2,1)S(1)}, bf16[256,1024]{1,0:T(8,128)(2,1)S(1)}, f32[16384,128]{1,0:T(8,128)S(1)}, f32[1024,1024]{1,0:T(8,128)...) custom-call(bf16[128,1024]{1,0:T(8,128)(2,1)} %cot_in.1, bf16[128,1024]{1,0:T(8,128)(2,1)} %saved_in.1, ...), custom_call_target="tpu_custom_call" | custom-call | tf_op jit(solution)/shard_map/mixer_backward/pallas_call | solution.py:487
  124.9 4.9 %write_out.1 = (bf16[128,1024]{1,0:T(8,128)(2,1)}, bf16[256,1024]{1,0:T(8,128)(2,1)}, f32[16384,128]{1,0:T(8,128)}, f32[1024,1024]{1,0:T(8,128)}) custom-call(bf16[128,1024]{1,0:T(8,128)(2,1)S(1)} %get-tuple-element.14.ig, bf16[256,1024]{1,0:T(8,128)(2,1)S(1)} %get-tuple-element.15.sg, f32[16384,128]{1,0:T(8,128)S(1)} %get-tuple-element.16.iwg, ...), custom_call_target="tpu_custom_call" | custom-call | tf_op jit(solution)/shard_map/write_out/pallas_call | solution.py:521

commit v6 on v5

--- a/solution.py
+++ b/solution.py
@@ -483,10 +483,11 @@
         return pltpu.VMEM((*shape, 1024), BF16)
 
     results = ((128, 1024), BF16), ((256, 1024), BF16), ((16384, 128), F32), ((1024, 1024), F32)
+    kept = results[:2] + (((16400, 128), F32),) + results[3:]
     passed = (((2, 8, 128, 1024), BF16),) * 2
     held = pl.pallas_call(
         kernel,
-        out_shape=[pltpu.VMEM(shape, dtype) for shape, dtype in results + passed],
+        out_shape=[pltpu.VMEM(shape, dtype) for shape, dtype in kept + passed],
         in_specs=[anywhere] * 7,
         out_specs=[pl.BlockSpec(memory_space=pltpu.VMEM)] * 6,
         scratch_shapes=[

time: 132 us -> 132 us (level)
  no operation moved by 1% of the time
where the time goes in v6:
time: 132 us; the launch traced here: 130 us
  Pallas kernels  129 us (98%)
    pallas_call x1, Pallas kernels, per_device(): pl.pallas_call(kernel, out_shape=[pltpu.VMEM(shape, dtype) for shape, dty...  124 us
    pallas_call x1, Pallas kernels, per_device(): pl.pallas_call(write_out, out_shape=[jax.ShapeDtypeStruct(shape, dtype) f...  4.91 us

profile of v6, /device:TPU:6, one launch (start us, length us, event | category | flops | bytes accessed | tf_op | source)
XLA Modules:
  0.0 130.0 jit_solution(16531572718779699128)
XLA Ops:
  0.6 124.3 %mixer_backward.1 = (bf16[128,1024]{1,0:T(8,128)(2,1)S(1)}, bf16[256,1024]{1,0:T(8,128)(2,1)S(1)}, f32[16400,128]{1,0:T(8,128)S(1)}, f32[1024,1024]{1,0:T(8,128)...) custom-call(bf16[128,1024]{1,0:T(8,128)(2,1)} %cot_in.1, bf16[128,1024]{1,0:T(8,128)(2,1)} %saved_in.1, ...), custom_call_target="tpu_custom_call" | custom-call | tf_op jit(solution)/shard_map/mixer_backward/pallas_call | solution.py:488
  124.9 4.9 %write_out.1 = (bf16[128,1024]{1,0:T(8,128)(2,1)}, bf16[256,1024]{1,0:T(8,128)(2,1)}, f32[16384,128]{1,0:T(8,128)}, f32[1024,1024]{1,0:T(8,128)}) custom-call(bf16[128,1024]{1,0:T(8,128)(2,1)S(1)} %get-tuple-element.14.ig, bf16[256,1024]{1,0:T(8,128)(2,1)S(1)} %get-tuple-element.15.sg, f32[16400,128]{1,0:T(8,128)S(1)} %get-tuple-element.16.iwg, ...), custom_call_target="tpu_custom_call" | custom-call | tf_op jit(solution)/shard_map/write_out/pallas_call | solution.py:522
